TPU v7x, 512 devices: a whole 4x8x8 slice. The times are simulated.
512 devices in a mesh: role: 4 (over x), ep: 64 (over z, y), dp: 2 (over core).
Axes of the slice: x: 4, y: 8, z: 8, core: 2. Of those that a mesh axis runs over, the one named last changes fastest.
Arguments:
- latents: bfloat16 [16, 4096, 1536], P(('role', 'dp'), 'ep'), may hold values from -6 to 6
- noise: bfloat16 [1, 16, 4096, 1536], P(None, ('role', 'dp'), 'ep'), may hold values from -6 to 6
- expert_ids: int32 [1, 16, 4096, 6], P(None, ('role', 'dp'), 'ep'), may hold values from 0 to 63, all different within a row; in each aligned block of 64 rows (0 to 63, 64 to 127, ..., all dimensions but the last counted through in order) at most 7 rows name the same one
- gate_values: float32 [1, 16, 4096, 6], P(None, ('role', 'dp'), 'ep'), may hold values from 0.1 to 1
- advantages: float32 [16], P(('role', 'dp')), may hold values from -4 to 4
- expert_pair: bfloat16 [64, 2, 768, 1536], P('ep', None, ('role', 'dp')), may hold values from -6 to 6
Outputs:
- final_latents: bfloat16 [16, 4096, 1536], P(('role', 'dp'), 'ep')
- new_down: bfloat16 [64, 768, 1536], P('ep')
Inputs may be any that keep to these rules, and one draw needn't show every extreme that they name: `expert_ids`: each row names 6 different experts. In every aligned block of 64 rows (steps, images and tokens taken together in order; one index of ep holds one block of an image at a step) no expert is named more than 7 times, a bound that some block reaches.
All inputs are finite; a program needn't handle non-finite values.
Results may differ from a plain program's by a relative error of at most 0.008.
Values may be sent and summed in bfloat16 or wider, within the bound.
A program may use at most 128 MiB of HBM per device.

v0:
```python
import math
import jax
import jax.numpy as jnp
from jax import lax
from jax.sharding import PartitionSpec as P

CAP = 7


def coefficients(section):
    moment = 0.95 - 0.4 * section
    noise_level = 0.3 * math.sqrt(moment / (1.0 - moment))
    factor = noise_level * noise_level / (2.0 * moment)
    keep_gain = 1.0 - 0.4 * factor
    drift_gain = -0.4 * (1.0 + factor * (1.0 - moment))
    noise_gain = noise_level * math.sqrt(0.4)
    return (keep_gain, drift_gain, noise_gain)


def slot_matrices(picked, weights, experts, capacity):
    image_count, tokens, chosen_count = picked.shape
    flat_ids = picked.reshape(image_count, tokens * chosen_count)
    onehot = (flat_ids[..., None] == jnp.arange(experts, dtype=jnp.int32)).astype(jnp.int32)
    ranks = jnp.cumsum(onehot, axis=1) - 1
    placed = jnp.sum(ranks * onehot, axis=2)
    image_column = jnp.arange(image_count, dtype=jnp.int32)[:, None]
    slot_ids = (flat_ids * image_count + image_column) * capacity + placed
    slot_ids = slot_ids.reshape(image_count * tokens, chosen_count)
    total_slots = experts * image_count * capacity
    marked = (slot_ids[..., None] == jnp.arange(total_slots, dtype=jnp.int32)).astype(jnp.float32)
    selected = jnp.sum(marked, axis=1)
    flat_weights = weights.reshape(image_count * tokens, chosen_count)
    slot_gate = jnp.sum(jnp.sum(marked * flat_weights[..., None], axis=1), axis=0)
    return (slot_ids, selected, slot_gate, flat_weights)


def expert_pass(inputs, w_up, w_down):
    width = inputs.shape[-1]
    hidden_units = w_up.shape[1]
    pre_act = jnp.einsum("jlcd,lhd->jlch", inputs, w_up, preferred_element_type=jnp.float32) * (
        1.0 / math.sqrt(width)
    )
    hidden = jax.nn.gelu(pre_act, approximate=True).astype(jnp.bfloat16)
    output = jnp.einsum("jlch,lhd->jlcd", hidden, w_down, preferred_element_type=jnp.float32) * (
        1.0 / math.sqrt(hidden_units)
    )
    returned = lax.all_to_all(
        output.astype(jnp.bfloat16), "ep", split_axis=0, concat_axis=0, tiled=True
    )
    return (returned, hidden)


def per_device(latents, noise, expert_ids, gate_values, advantages, expert_pair):
    ep_size = lax.axis_size("ep")
    group_size = lax.axis_size("role") * lax.axis_size("dp")
    local_experts = expert_pair.shape[0]
    experts = local_experts * ep_size
    capacity = CAP
    image_count = latents.shape[0]
    tok_count = latents.shape[1]
    width = latents.shape[2]
    top_count = expert_ids.shape[3]
    total_slots = experts * image_count * capacity
    full_pair = lax.all_gather(expert_pair, ("role", "dp"), axis=2, tiled=True)
    w_up = full_pair[:, 0]
    w_down = full_pair[:, 1]
    hidden_units = full_pair.shape[2]
    current = latents.reshape(image_count * tok_count, width)
    image_of_slot = jnp.arange(total_slots, dtype=jnp.int32) // capacity % image_count
    keep_gain, drift_gain, noise_gain = coefficients(0)
    slot_ids, selected, slot_gate, flat_weights = slot_matrices(
        expert_ids[0], gate_values[0], experts, capacity
    )
    selected_half = selected.astype(jnp.bfloat16)
    noise_now = noise[0].reshape(image_count * tok_count, width)
    slot_latent = jnp.einsum(
        "ts,td->sd", selected_half, current, preferred_element_type=jnp.float32
    )
    slot_latent = slot_latent.astype(jnp.bfloat16).reshape(
        ep_size, local_experts, image_count * capacity, width
    )
    slot_noise = jnp.einsum(
        "ts,td->sd", selected_half, noise_now, preferred_element_type=jnp.float32
    )
    image_factor = advantages * (drift_gain / noise_gain)
    slot_scale = slot_gate * image_factor[image_of_slot]
    home_cot = (
        (slot_scale[:, None] * slot_noise)
        .astype(jnp.bfloat16)
        .reshape(ep_size, local_experts, image_count * capacity, width)
    )
    returned, hidden = expert_pass(
        lax.all_to_all(slot_latent, "ep", split_axis=0, concat_axis=0, tiled=True), w_up, w_down
    )
    returned, hidden, cotangent = (
        returned,
        hidden,
        lax.all_to_all(home_cot, "ep", split_axis=0, concat_axis=0, tiled=True),
    )
    back_rows = returned.reshape(total_slots, width)
    taken = jnp.take(back_rows, slot_ids, axis=0)
    velocity = jnp.sum(flat_weights[..., None] * taken.astype(jnp.float32), axis=1)
    moved = (
        keep_gain * current.astype(jnp.float32)
        + drift_gain * velocity
        + noise_gain * noise_now.astype(jnp.float32)
    )
    current = moved.astype(jnp.bfloat16)
    kept_hidden = [hidden]
    kept_cot = [cotangent]
    rate = 10.0 / math.sqrt(tok_count * ep_size * top_count * image_count * group_size / experts)
    total = jnp.zeros((hidden_units, local_experts, width), jnp.float32)
    for hidden, cotangent in zip(kept_hidden, kept_cot):
        total = jnp.einsum("jlch,jlcd->hld", hidden, cotangent, preferred_element_type=jnp.float32)
    summed = lax.psum(
        (total * (1.0 / math.sqrt(hidden_units)))
        .reshape(hidden_units, local_experts * width)
        .astype(jnp.bfloat16),
        ("role", "dp"),
    ).astype(jnp.float32)
    summed = jnp.transpose(summed.reshape(hidden_units, local_experts, width), (1, 0, 2))
    new_down = (w_down.astype(jnp.float32) + rate * summed).astype(jnp.bfloat16)
    return (current.reshape(image_count, tok_count, width), new_down)


def solution(mesh):
    in_specs = (
        P(("role", "dp"), "ep", None),
        P(None, ("role", "dp"), "ep", None),
        P(None, ("role", "dp"), "ep", None),
        P(None, ("role", "dp"), "ep", None),
        P(("role", "dp")),
        P("ep", None, ("role", "dp"), None),
    )
    out_specs = (P(("role", "dp"), "ep", None), P("ep", None, None))
    return jax.shard_map(
        per_device, mesh=mesh, in_specs=in_specs, out_specs=out_specs, check_vma=False
    )
```

profile of v0, /device:TPU:8, one launch (start us, length us, event | category | flops | bytes accessed | tf_op | source)
XLA Modules:
  0.0 347.8 jit_solution(13016884792895209371)
XLA Ops:
  7.2 0.8 copy.62
  8.0 0.1 eq.44
  8.1 0.1 eq.40
  8.2 0.7 broadcast_multiply_fusion.1
  9.0 1.8 reduce-window.6
  10.8 0.1 slice.21
  10.9 0.1 copy.64
  11.0 0.1 fusion.26
  11.2 0.1 reduce_sum.45
  11.3 0.1 copy.67
  11.4 0.1 mul.180
  11.5 0.1 add.131
  11.6 0.8 mul.176
  12.3 0.6 compare_and_fusion
  12.9 0.6 select_reduce_fusion
  13.5 1.9 convolution_convert_fusion
  15.4 2.5 reshape.262
  17.9 16.9 %all-to-all-start = ((bf16[64,1,14,1536]{3,2,1,0:T(8,128)(2,1)}), bf16[64,1,14,1536]{3,2,1,0:T(8,128)(2,1)}, u32[]{:S(2)}, u32[]{:S(2)}) async-start(bf16[64,1,14,1536]{3,2,1,0:T(8,128)(2,1)} %bitcast.3), calls=%async_computation | async-start | bytes 6291456 | tf_op jit(solution)/shard_map/all_to_all | solution.py:93
  34.9 0.7 all-gather.2.cloned.1.call-update
  35.6 0.6 fusion.34
  36.2 1.3 fusion.30
  37.5 0.9 multiply_convert_fusion
  38.4 2.6 reshape.268
  41.0 73.6 %all-to-all-done = bf16[64,1,14,1536]{3,2,1,0:T(8,128)(2,1)} async-done(((bf16[64,1,14,1536]{3,2,1,0:T(8,128)(2,1)}), bf16[64,1,14,1536]{3,2,1,0:T(8,128)(2,1)}, u32[]{:S(2)}, u32[]{:S(2)}) %all-to-all-start) | async-done | bytes 2752544 | tf_op jit(solution)/shard_map/all_to_all | solution.py:93
  114.6 22.3 %all-to-all-start.2 = ((bf16[64,1,14,1536]{3,2,1,0:T(8,128)(2,1)}), bf16[64,1,14,1536]{3,2,1,0:T(8,128)(2,1)S(1)}, u32[]{:S(2)}, u32[]{:S(2)}) async-start(bf16[64,1,14,1536]{3,2,1,0:T(8,128)(2,1)} %bitcast.23), calls=%async_computation.2 | async-start | bytes 6291456 | tf_op jit(solution)/shard_map/all_to_all | solution.py:98
  136.9 8.1 %fusion.21 = bf16[64,14,768]{2,0,1:T(8,128)(2,1)S(1)} fusion(bf16[1,2,768,1536]{3,2,1,0:T(8,128)(2,1)} %all-gather.2.cloned.1.call-done, bf16[64,1,14,1536]{3,2,1,0:T(8,128)(2,1)} %all-to-all-done), kind=kOutput, calls=%fused_computation.31 | convolution fusion | flops 2120810496 | bytes 6881280 | tf_op jit(solution)/shard_map/jlcd,lhd->jlch/dot_general | solution.py:40
  145.0 2.3 fusion.1
  147.3 3.2 copy.71
  150.5 62.1 %all-to-all-done.2 = bf16[64,1,14,1536]{3,2,1,0:T(8,128)(2,1)S(1)} async-done(((bf16[64,1,14,1536]{3,2,1,0:T(8,128)(2,1)}), bf16[64,1,14,1536]{3,2,1,0:T(8,128)(2,1)S(1)}, u32[]{:S(2)}, u32[]{:S(2)}) %all-to-all-start.2) | async-done | bytes 2752544 | tf_op jit(solution)/shard_map/all_to_all | solution.py:98
  212.6 21.0 %all-to-all-start.1 = ((bf16[64,1,14,1536]{3,2,1,0:T(8,128)(2,1)}), bf16[64,1,14,1536]{3,2,1,0:T(8,128)(2,1)}, u32[]{:S(2)}, u32[]{:S(2)}) async-start(bf16[64,1,14,1536]{3,2,1,0:T(8,128)(2,1)} %copy.71), calls=%async_computation.1 | async-start | bytes 6291456 | tf_op jit(solution)/shard_map/all_to_all | solution.py:47
  233.6 0.3 all-reduce.2.cloned.1.call-start
  233.9 7.0 %fusion.2 = bf16[768,1536]{1,0:T(8,128)(2,1)} fusion(bf16[64,14,768]{2,0,1:T(8,128)(2,1)} %copy-done.5, bf16[64,1,14,1536]{3,2,1,0:T(8,128)(2,1)S(1)} %all-to-all-done.2), kind=kOutput, calls=%fused_computation.10 | convolution fusion | flops 2116288512 | bytes 6488064 | tf_op jit(solution)/shard_map/jlch,jlcd->hld/dot_general | solution.py:114
  240.9 0.1 reduce_sum.47
  241.1 0.1 mul.198
  241.2 0.7 copy.61
  241.9 0.1 copy.72
  242.0 0.7 compare_select_fusion.1
  242.7 0.1 copy.73
  242.8 0.1 reshape.272
  242.9 0.8 copy.68
  243.7 76.6 %all-reduce.2.cloned.1.call-done = bf16[768,1536]{1,0:T(8,128)(2,1)} async-done(((bf16[768,1536]{1,0:T(8,128)(2,1)}), bf16[768,1536]{1,0:T(8,128)(2,1)}) %all-reduce.2.cloned.1.call-update) | async-done | bytes 2359312 | tf_op jit(solution)/shard_map/psum | solution.py:115
  320.3 4.5 %fusion.16 = bf16[1,768,1536]{2,1,0:T(8,128)(2,1)} fusion(bf16[768,1536]{1,0:T(8,128)(2,1)} %all-reduce.2.cloned.1.call-done, bf16[1,2,768,1536]{3,2,1,0:T(8,128)(2,1)} %all-gather.2.cloned.1.call-done), kind=kLoop, calls=%fused_computation.27 | loop fusion | flops 5898240 | bytes 7077888 | tf_op jit(solution)/shard_map/convert_element_type | solution.py:122
  324.8 3.8 %reshape.267 = bf16[896,1536]{1,0:T(8,128)(2,1)S(1)} reshape(bf16[64,1,14,1536]{3,2,1,0:T(8,128)(2,1)} %all-to-all-done.1) | data formatting | bytes 5505024 | tf_op jit(solution)/shard_map/reshape | solution.py:100
  328.6 3.8 %gather_fusion = bf16[768,1536]{1,0:T(8,128)(2,1)} fusion(bf16[896,1536]{1,0:T(8,128)(2,1)S(1)} %reshape.267, s32[1024]{0:T(1024)S(1)} %pad_clamp_fusion), kind=kCustom, calls=%fused_computation | custom fusion | bytes 4721664 | tf_op jit(solution)/shard_map/jit(_take)/gather | solution.py:101
  332.4 3.5 %reshape.271 = bf16[128,6,1536]{2,1,0:T(8,128)(2,1)S(1)} reshape(bf16[768,1536]{1,0:T(8,128)(2,1)} %gather_fusion) | data formatting | bytes 4718592 | tf_op jit(solution)/shard_map/jit(_take)/gather | solution.py:101
  336.0 4.0 %multiply_reduce_fusion = f32[128,1536]{1,0:T(8,128)S(1)} fusion(bf16[128,6,1536]{2,1,0:T(8,128)(2,1)S(1)} %reshape.271, f32[128,6]{1,0:T(8,128)} %copy.61, pred[128,6]{1,0:T(8,128)(4,1)S(1)} %copy.68), kind=kLoop, calls=%fused_computation.1 | loop fusion | flops 4521984 | bytes 3149568 | tf_op jit(solution)/shard_map/reduce_sum | solution.py:102
  340.0 0.1 broadcast_multiply_fusion
  340.1 0.9 fusion.24
  (24 shorter events, 0.2 us)
Async XLA Ops:
  11.6 6.4 %copy-start.3 = (s32[128]{0:T(128)}, s32[128]{0:T(128)S(1)}, u32[]{:S(2)}) copy-start(s32[128]{0:T(128)S(1)} %add.131) | copy-start | bytes 1540
  17.9 17.6 %copy-start.4 = (f32[2]{0:T(128)S(1)}, f32[2]{0:T(128)}, u32[]{:S(2)}) copy-start(f32[2]{0:T(128)} %param.10) | copy-start | bytes 28
  17.9 19.6 %copy-start = (bf16[1,2,64,1536]{3,2,1,0:T(8,128)(2,1)S(1)}, bf16[1,2,64,1536]{3,2,1,0:T(8,128)(2,1)}, u32[]{:S(2)}) copy-start(bf16[1,2,64,1536]{3,2,1,0:T(8,128)(2,1)} %param.7) | copy-start | bytes 1179652
  17.9 96.6 %all-to-all-start = ((bf16[64,1,14,1536]{3,2,1,0:T(8,128)(2,1)}), bf16[64,1,14,1536]{3,2,1,0:T(8,128)(2,1)}, u32[]{:S(2)}, u32[]{:S(2)}) async-start(bf16[64,1,14,1536]{3,2,1,0:T(8,128)(2,1)} %bitcast.3), calls=%async_computation | async-start | bytes 6291456 | tf_op jit(solution)/shard_map/all_to_all | solution.py:93
  34.8 102.1 %all-gather.2.cloned.1.call-start = ((), (), s32[]{:S(2)}) async-start(), calls=%async_computation.3 | async-start | bytes 5308416 | tf_op jit(solution)/shard_map/all_gather | solution.py:64
  114.6 98.0 %all-to-all-start.2 = ((bf16[64,1,14,1536]{3,2,1,0:T(8,128)(2,1)}), bf16[64,1,14,1536]{3,2,1,0:T(8,128)(2,1)S(1)}, u32[]{:S(2)}, u32[]{:S(2)}) async-start(bf16[64,1,14,1536]{3,2,1,0:T(8,128)(2,1)} %bitcast.23), calls=%async_computation.2 | async-start | bytes 6291456 | tf_op jit(solution)/shard_map/all_to_all | solution.py:98
  136.9 8.1 %copy-start.2 = (bf16[1,2,768,1536]{3,2,1,0:T(8,128)(2,1)S(1)}, bf16[1,2,768,1536]{3,2,1,0:T(8,128)(2,1)}, u32[]{:S(2)}) copy-start(bf16[1,2,768,1536]{3,2,1,0:T(8,128)(2,1)} %all-gather.2.cloned.1.call-done) | copy-start | bytes 14155780
  145.0 2.3 copy-start.5
  212.6 112.2 %all-to-all-start.1 = ((bf16[64,1,14,1536]{3,2,1,0:T(8,128)(2,1)}), bf16[64,1,14,1536]{3,2,1,0:T(8,128)(2,1)}, u32[]{:S(2)}, u32[]{:S(2)}) async-start(bf16[64,1,14,1536]{3,2,1,0:T(8,128)(2,1)} %copy.71), calls=%async_computation.1 | async-start | bytes 6291456 | tf_op jit(solution)/shard_map/all_to_all | solution.py:47
  233.6 86.7 %all-reduce.2.cloned.1.call-start = ((), (), s32[]{:S(2)}) async-start(), calls=%async_computation.4 | async-start | bytes 4718592 | tf_op jit(solution)/shard_map/psum | solution.py:115
  336.0 4.1 %copy-start.1 = (bf16[2,64,1536]{2,1,0:T(8,128)(2,1)S(1)}, bf16[2,64,1536]{2,1,0:T(8,128)(2,1)}, u32[]{:S(2)}) copy-start(bf16[2,64,1536]{2,1,0:T(8,128)(2,1)} %param.6) | copy-start | bytes 1179652
Sparse Core Ops, SparseCore 0:
  37.8 40.3 all-gather.1
  241.1 79.2 all-reduce.1
where the time goes:
time: 349 us; the launch traced here: 348 us
  waiting for transfers between devices  213 us (61%)
  starting transfers between devices  60.5 us (17%)
  local copies, waits for them, and re-layouts  24.5 us (7%)
  matrix products  20.2 us (6%)
  other arithmetic  15.4 us (4%)
  between operations  14.3 us (4%)
    psum x1, waiting for transfers between devices, per_device(): lax.psum((total * (1.0 / math.sqrt(hidden_units))).reshape(hidden_units,...  76.6 us
    all_to_all x1, waiting for transfers between devices, per_device(): lax.all_to_all(slot_latent, 'ep', split_axis=0, concat_axis=0, tiled=True)  73.6 us
    all_to_all x1, waiting for transfers between devices, per_device(): lax.all_to_all(home_cot, 'ep', split_axis=0, concat_axis=0, tiled=True)  62.1 us
    all_to_all x1, starting transfers between devices, per_device(): lax.all_to_all(home_cot, 'ep', split_axis=0, concat_axis=0, tiled=True)  22.3 us
    all_to_all x1, starting transfers between devices, expert_pass(): lax.all_to_all(output.astype(jnp.bfloat16), 'ep', split_axis=0, concat_ax...  21 us
    all_to_all x1, starting transfers between devices, per_device(): lax.all_to_all(slot_latent, 'ep', split_axis=0, concat_axis=0, tiled=True)  16.9 us
    dot_general x1, matrix products, expert_pass(): jnp.einsum('jlcd,lhd->jlch', inputs, w_up, preferred_element_type=jnp.flo...  8.06 us
    gather x2, local copies, waits for them, and re-layouts, per_device(): taken = jnp.take(back_rows, slot_ids, axis=0)  7.35 us
  transfers between devices with their start and end apart: 5, of which 3 were waited for; matrix products, arithmetic and copies ran while one was open for 10% of the time, Pallas kernels for 0%

commit v1 on v0

--- a/solution.py
+++ b/solution.py
@@ -5,6 +5,11 @@
 from jax.sharding import PartitionSpec as P
 
 CAP = 7
+
+
+def one_after_other(array, first, second):
+    partial = lax.psum(array, first)
+    return lax.psum(partial, second)
 
 
 def coefficients(section):
@@ -112,11 +117,12 @@
     total = jnp.zeros((hidden_units, local_experts, width), jnp.float32)
     for hidden, cotangent in zip(kept_hidden, kept_cot):
         total = jnp.einsum("jlch,jlcd->hld", hidden, cotangent, preferred_element_type=jnp.float32)
-    summed = lax.psum(
+    summed = one_after_other(
         (total * (1.0 / math.sqrt(hidden_units)))
         .reshape(hidden_units, local_experts * width)
         .astype(jnp.bfloat16),
-        ("role", "dp"),
+        "dp",
+        "role",
     ).astype(jnp.float32)
     summed = jnp.transpose(summed.reshape(hidden_units, local_experts, width), (1, 0, 2))
     new_down = (w_down.astype(jnp.float32) + rate * summed).astype(jnp.bfloat16)

time: 349 us -> 386 us (1.11)
  the two profiles are of different devices: /device:TPU:8 before, /device:TPU:1 now
where the time goes in v1:
time: 386 us; the launch traced here: 385 us
  waiting for transfers between devices  246 us (64%)
  starting transfers between devices  66.5 us (17%)
  local copies, waits for them, and re-layouts  23.9 us (6%)
  matrix products  20.2 us (5%)
  other arithmetic  14.7 us (4%)
  between operations  14 us (4%)
    psum x1, waiting for transfers between devices, one_after_other(): return lax.psum(partial, second)  74.6 us
    all_to_all x1, waiting for transfers between devices, per_device(): lax.all_to_all(slot_latent, 'ep', split_axis=0, concat_axis=0, tiled=True)  67 us
    all_to_all x1, waiting for transfers between devices, per_device(): lax.all_to_all(home_cot, 'ep', split_axis=0, concat_axis=0, tiled=True)  61.7 us
    psum x1, waiting for transfers between devices, one_after_other(): partial = lax.psum(array, first)  41.9 us
    all_to_all x1, starting transfers between devices, per_device(): lax.all_to_all(home_cot, 'ep', split_axis=0, concat_axis=0, tiled=True)  27.8 us
    all_to_all x1, starting transfers between devices, expert_pass(): lax.all_to_all(output.astype(jnp.bfloat16), 'ep', split_axis=0, concat_ax...  20.9 us
    all_to_all x1, starting transfers between devices, per_device(): lax.all_to_all(slot_latent, 'ep', split_axis=0, concat_axis=0, tiled=True)  17.5 us
    dot_general x1, matrix products, expert_pass(): jnp.einsum('jlcd,lhd->jlch', inputs, w_up, preferred_element_type=jnp.flo...  8.06 us
  transfers between devices with their start and end apart: 6, of which 4 were waited for; matrix products, arithmetic and copies ran while one was open for 8% of the time, Pallas kernels for 0%

profile of v1, /device:TPU:1, one launch (start us, length us, event | category | flops | bytes accessed | tf_op | source)
XLA Modules:
  0.0 385.1 jit_solution(14806151401202601418)
XLA Ops:
  7.2 0.8 copy.62
  8.0 0.1 eq.44
  8.1 0.1 eq.40
  8.2 0.7 broadcast_multiply_fusion.1
  9.0 1.8 reduce-window.6
  10.8 0.1 slice.21
  10.9 0.1 copy.64
  11.0 0.1 fusion.26
  11.2 0.1 reduce_sum.45
  11.3 0.1 copy.67
  11.4 0.1 mul.180
  11.5 0.1 add.133
  11.6 0.8 mul.176
  12.3 0.5 compare_and_fusion
  12.9 0.6 select_reduce_fusion
  13.5 1.9 convolution_convert_fusion
  15.4 2.5 reshape.262
  17.9 17.5 %all-to-all-start = ((bf16[64,1,14,1536]{3,2,1,0:T(8,128)(2,1)}), bf16[64,1,14,1536]{3,2,1,0:T(8,128)(2,1)}, u32[]{:S(2)}, u32[]{:S(2)}) async-start(bf16[64,1,14,1536]{3,2,1,0:T(8,128)(2,1)} %bitcast.3), calls=%async_computation | async-start | bytes 6291456 | tf_op jit(solution)/shard_map/all_to_all | solution.py:98
  35.4 0.7 all-gather.2.cloned.1.call-update
  36.2 0.6 fusion.34
  36.7 1.3 fusion.30
  38.1 0.9 multiply_convert_fusion
  39.0 2.6 reshape.268
  41.6 67.0 %all-to-all-done = bf16[64,1,14,1536]{3,2,1,0:T(8,128)(2,1)} async-done(((bf16[64,1,14,1536]{3,2,1,0:T(8,128)(2,1)}), bf16[64,1,14,1536]{3,2,1,0:T(8,128)(2,1)}, u32[]{:S(2)}, u32[]{:S(2)}) %all-to-all-start) | async-done | bytes 2752544 | tf_op jit(solution)/shard_map/all_to_all | solution.py:98
  108.6 27.8 %all-to-all-start.2 = ((bf16[64,1,14,1536]{3,2,1,0:T(8,128)(2,1)}), bf16[64,1,14,1536]{3,2,1,0:T(8,128)(2,1)S(1)}, u32[]{:S(2)}, u32[]{:S(2)}) async-start(bf16[64,1,14,1536]{3,2,1,0:T(8,128)(2,1)} %bitcast.23), calls=%async_computation.2 | async-start | bytes 6291456 | tf_op jit(solution)/shard_map/all_to_all | solution.py:103
  136.5 8.1 %fusion.21 = bf16[64,14,768]{2,0,1:T(8,128)(2,1)S(1)} fusion(bf16[1,2,768,1536]{3,2,1,0:T(8,128)(2,1)} %all-gather.2.cloned.1.call-done, bf16[64,1,14,1536]{3,2,1,0:T(8,128)(2,1)} %all-to-all-done), kind=kOutput, calls=%fused_computation.31 | convolution fusion | flops 2120810496 | bytes 6881280 | tf_op jit(solution)/shard_map/jlcd,lhd->jlch/dot_general | solution.py:45
  144.5 2.3 fusion.1
  146.8 3.2 copy.71
  150.0 61.7 %all-to-all-done.2 = bf16[64,1,14,1536]{3,2,1,0:T(8,128)(2,1)S(1)} async-done(((bf16[64,1,14,1536]{3,2,1,0:T(8,128)(2,1)}), bf16[64,1,14,1536]{3,2,1,0:T(8,128)(2,1)S(1)}, u32[]{:S(2)}, u32[]{:S(2)}) %all-to-all-start.2) | async-done | bytes 2752544 | tf_op jit(solution)/shard_map/all_to_all | solution.py:103
  211.7 20.9 %all-to-all-start.1 = ((bf16[64,1,14,1536]{3,2,1,0:T(8,128)(2,1)}), bf16[64,1,14,1536]{3,2,1,0:T(8,128)(2,1)}, u32[]{:S(2)}, u32[]{:S(2)}) async-start(bf16[64,1,14,1536]{3,2,1,0:T(8,128)(2,1)} %copy.71), calls=%async_computation.1 | async-start | bytes 6291456 | tf_op jit(solution)/shard_map/all_to_all | solution.py:52
  232.7 7.0 %fusion.2 = bf16[768,1536]{1,0:T(8,128)(2,1)} fusion(bf16[64,14,768]{2,0,1:T(8,128)(2,1)} %copy-done.7, bf16[64,1,14,1536]{3,2,1,0:T(8,128)(2,1)S(1)} %all-to-all-done.2), kind=kOutput, calls=%fused_computation.10 | convolution fusion | flops 2116288512 | bytes 6488064 | tf_op jit(solution)/shard_map/jlch,jlcd->hld/dot_general | solution.py:119
  239.7 0.3 all-reduce.5.cloned.1.call-start
  240.0 41.9 %all-reduce.3.cloned.1.call-done = bf16[768,1536]{1,0:T(8,128)(2,1)} async-done(((bf16[768,1536]{1,0:T(8,128)(2,1)}), bf16[768,1536]{1,0:T(8,128)(2,1)}) %all-reduce.3.cloned.1.call-update) | async-done | bytes 2359312 | tf_op jit(solution)/shard_map/psum | solution.py:11
  281.9 0.1 reduce_sum.47
  282.0 0.1 mul.198
  282.1 0.7 copy.61
  282.8 0.1 copy.72
  282.9 0.1 copy.73
  283.1 0.1 reshape.272
  283.2 0.1 copy.68
  283.4 74.6 %all-reduce.5.cloned.1.call-done = bf16[768,1536]{1,0:T(8,128)(2,1)} async-done(((bf16[768,1536]{1,0:T(8,128)(2,1)}), bf16[768,1536]{1,0:T(8,128)(2,1)}) %all-reduce.5.cloned.1.call-update) | async-done | bytes 2359312 | tf_op jit(solution)/shard_map/psum | solution.py:12
  357.9 4.5 %fusion.16 = bf16[1,768,1536]{2,1,0:T(8,128)(2,1)} fusion(bf16[768,1536]{1,0:T(8,128)(2,1)} %all-reduce.5.cloned.1.call-done, bf16[1,2,768,1536]{3,2,1,0:T(8,128)(2,1)} %all-gather.2.cloned.1.call-done), kind=kLoop, calls=%fused_computation.27 | loop fusion | flops 5898240 | bytes 7077888 | tf_op jit(solution)/shard_map/convert_element_type | solution.py:128
  362.4 3.8 reshape.267
  366.2 3.8 gather_fusion
  370.0 3.5 reshape.271
  373.6 4.0 %multiply_reduce_fusion = f32[128,1536]{1,0:T(8,128)S(1)} fusion(bf16[128,6,1536]{2,1,0:T(8,128)(2,1)S(1)} %reshape.271, f32[128,6]{1,0:T(8,128)} %copy.61, pred[128,6]{1,0:T(8,128)(4,1)S(1)} %copy.68), kind=kLoop, calls=%fused_computation.1 | loop fusion | flops 4521984 | bytes 3149568 | tf_op jit(solution)/shard_map/reduce_sum | solution.py:107
  377.6 0.1 broadcast_multiply_fusion
  377.7 0.9 fusion.24
  (31 shorter events, 0.2 us)
Async XLA Ops:
  11.6 6.3 %copy-start.4 = (s32[128]{0:T(128)}, s32[128]{0:T(128)S(1)}, u32[]{:S(2)}) copy-start(s32[128]{0:T(128)S(1)} %add.133) | copy-start | bytes 1540
  17.9 18.3 %copy-start.6 = (f32[2]{0:T(128)S(1)}, f32[2]{0:T(128)}, u32[]{:S(2)}) copy-start(f32[2]{0:T(128)} %param.10) | copy-start | bytes 28
  17.9 20.2 %copy-start = (bf16[1,2,64,1536]{3,2,1,0:T(8,128)(2,1)S(1)}, bf16[1,2,64,1536]{3,2,1,0:T(8,128)(2,1)}, u32[]{:S(2)}) copy-start(bf16[1,2,64,1536]{3,2,1,0:T(8,128)(2,1)} %param.7) | copy-start | bytes 1179652
  17.9 90.7 %all-to-all-start = ((bf16[64,1,14,1536]{3,2,1,0:T(8,128)(2,1)}), bf16[64,1,14,1536]{3,2,1,0:T(8,128)(2,1)}, u32[]{:S(2)}, u32[]{:S(2)}) async-start(bf16[64,1,14,1536]{3,2,1,0:T(8,128)(2,1)} %bitcast.3), calls=%async_computation | async-start | bytes 6291456 | tf_op jit(solution)/shard_map/all_to_all | solution.py:98
  35.4 101.0 %all-gather.2.cloned.1.call-start = ((), (), s32[]{:S(2)}) async-start(), calls=%async_computation.3 | async-start | bytes 5308416 | tf_op jit(solution)/shard_map/all_gather | solution.py:69
  108.6 103.1 %all-to-all-start.2 = ((bf16[64,1,14,1536]{3,2,1,0:T(8,128)(2,1)}), bf16[64,1,14,1536]{3,2,1,0:T(8,128)(2,1)S(1)}, u32[]{:S(2)}, u32[]{:S(2)}) async-start(bf16[64,1,14,1536]{3,2,1,0:T(8,128)(2,1)} %bitcast.23), calls=%async_computation.2 | async-start | bytes 6291456 | tf_op jit(solution)/shard_map/all_to_all | solution.py:103
  136.4 8.1 %copy-start.2 = (bf16[1,2,768,1536]{3,2,1,0:T(8,128)(2,1)S(1)}, bf16[1,2,768,1536]{3,2,1,0:T(8,128)(2,1)}, u32[]{:S(2)}) copy-start(bf16[1,2,768,1536]{3,2,1,0:T(8,128)(2,1)} %all-gather.2.cloned.1.call-done) | copy-start | bytes 14155780
  144.5 2.3 copy-start.7
  211.7 150.7 %all-to-all-start.1 = ((bf16[64,1,14,1536]{3,2,1,0:T(8,128)(2,1)}), bf16[64,1,14,1536]{3,2,1,0:T(8,128)(2,1)}, u32[]{:S(2)}, u32[]{:S(2)}) async-start(bf16[64,1,14,1536]{3,2,1,0:T(8,128)(2,1)} %copy.71), calls=%async_computation.1 | async-start | bytes 6291456 | tf_op jit(solution)/shard_map/all_to_all | solution.py:52
  232.6 49.2 %all-reduce.3.cloned.1.call-start = ((), (), s32[]{:S(2)}) async-start(), calls=%async_computation.4 | async-start | bytes 4718592 | tf_op jit(solution)/shard_map/psum | solution.py:11
  239.7 43.2 %copy-start.5 = (s32[128]{0:T(128)S(1)}, s32[128]{0:T(128)}, u32[]{:S(2)}) copy-start(s32[128]{0:T(128)} %copy-done.4) | copy-start | bytes 1540
  239.7 43.5 %copy-start.3 = (pred[128,6]{0,1:T(8,128)(4,1)S(1)}, pred[128,6]{0,1:T(8,128)(4,1)}, u32[]{:S(2)}) copy-start(pred[128,6]{0,1:T(8,128)(4,1)} %get-tuple-element.4) | copy-start | bytes 2308
  239.7 118.2 %all-reduce.5.cloned.1.call-start = ((), (), s32[]{:S(2)}) async-start(), calls=%async_computation.5 | async-start | bytes 4718592 | tf_op jit(solution)/shard_map/psum | solution.py:12
  373.6 4.1 %copy-start.1 = (bf16[2,64,1536]{2,1,0:T(8,128)(2,1)S(1)}, bf16[2,64,1536]{2,1,0:T(8,128)(2,1)}, u32[]{:S(2)}) copy-start(bf16[2,64,1536]{2,1,0:T(8,128)(2,1)} %param.6) | copy-start | bytes 1179652
Sparse Core Ops, SparseCore 0:
  38.4 41.0 all-gather.1
  239.8 41.9 all-reduce.2
  284.3 73.5 all-reduce.4
